TPU v7x, 32 devices: a whole 2x2x4 slice. The times are simulated.
32 devices in a mesh: prow: 8 (over z, x), pcol: 2 (over y), zgrid: 2 (over core).
Axes of the slice: x: 2, y: 2, z: 4, core: 2. Of those that a mesh axis runs over, the one named last changes fastest.
Arguments:
- blocks: bfloat16 [8, 2, 2, 3, 40, 128, 128], P('prow', 'pcol', 'zgrid'), may hold values from -0.078125 to 0.078125
- sources: int32 [8, 2, 2, 3, 40], P('prow', 'pcol', 'zgrid'), may hold values from 0 to 1, as said below
- targets: int32 [8, 2, 2, 3, 40], P('prow', 'pcol', 'zgrid'), may hold values from 0 to 23, as said below
- counts: int32 [8, 2, 2, 3], P('prow', 'pcol', 'zgrid'), may hold values from 1 to 40, as said below
- given_sub: bfloat16 [8, 2, 2, 2, 128, 128], P('prow', 'pcol', 'zgrid'), may hold values from -6 to 6
- given_top: bfloat16 [8, 2, 2, 128, 128], P('prow', 'pcol'), may hold values from -6 to 6
- inverse_sub: bfloat16 [8, 2, 2, 2, 128, 128], P('prow', 'pcol', 'zgrid'), as said below
- inverse_top: bfloat16 [8, 2, 2, 128, 128], P('prow', 'pcol'), as said below
Outputs:
- solved_sub: bfloat16 [8, 2, 2, 2, 128, 128], P('prow', 'pcol', 'zgrid')
- solved_top: bfloat16 [8, 2, 2, 128, 128], P('prow', 'pcol')
Inputs may be any that keep to these rules, and one draw needn't show every extreme that they name: `sources`: column of the source supernode of a slot. `targets`: a slot of source level l aims at a level t = value // 8 + 1 above l and the row value % 8. `counts`: on some device of each source level all 40 slots are live. `inverse_sub`: unit lower triangular. `inverse_top`: unit lower triangular.
All inputs are finite; a program needn't handle non-finite values.
Results may differ from a plain program's by a relative error of at most 0.023.
Values may be sent and summed in bfloat16 or wider, within the bound.
No kernel may reach another device: no remote copies, remote signals or barrier semaphores. Data moves between devices by JAX's collectives and lax.ppermute only.
A program may use at most 64 MiB of HBM per device.

v0:
```python
import functools

import jax
import jax.numpy as jnp
from jax import lax
from jax.experimental import pallas as pl
from jax.experimental.pallas import tpu as pltpu
from jax.sharding import PartitionSpec as P

slot_group = 8
field = 10
field_mask = (1 << field) - 1
pairs = ((0, 1), (0, 2), (0, 3), (1, 2), (1, 3), (2, 3))
params = pltpu.CompilerParams(vmem_limit_bytes=24 * 1024 * 1024)
vmem = pl.BlockSpec(memory_space=pltpu.VMEM)
smem = pl.BlockSpec(memory_space=pltpu.SMEM)
hbm = pl.BlockSpec(memory_space=pltpu.HBM)
anywhere = pl.BlockSpec(memory_space=pl.ANY)


def sibling_values(value, layers):
    cols = lax.axis_size("pcol")
    depth = lax.axis_size("zgrid")
    found = []
    for k in range(cols):
        if k == 0 and layers == 0:
            found.append(value)
            continue
        moves = []
        for c in range(cols):
            for z in range(depth):
                target = ((c - k) % cols) * depth + (z - layers) % depth
                moves.append((c * depth + z, target))
        found.append(lax.ppermute(value, ("pcol", "zgrid"), moves))
    return found


def from_other_core(value):
    return lax.ppermute(value, "zgrid", [(0, 1), (1, 0)])


def in_hbm(value):
    return pltpu.with_memory_space_constraint(value, pltpu.HBM)


def plan_kernel(row_count, cols, sources_in, targets_in, counts_in, blocks, plan, staged, *scratch):
    sources, targets, counts, semaphores = scratch
    loads = [
        pltpu.make_async_copy(sources_in, sources, semaphores.at[0]),
        pltpu.make_async_copy(targets_in, targets, semaphores.at[1]),
        pltpu.make_async_copy(counts_in, counts, semaphores.at[2]),
    ]
    for load in loads:
        load.start()
    stage = pltpu.make_async_copy(blocks.at[0], staged, semaphores.at[3])
    stage.start()
    for load in loads:
        load.wait()
    me = lax.axis_index("pcol")
    spare = row_count << field
    for level in range(3):
        first_list = pairs.index((level, level + 1))
        lists = 3 - level

        def one_slot(slot, found):
            target = targets[level, 0, slot]
            higher = [(target >= (level + j) * row_count).astype(jnp.int32) for j in range(1, lists)]
            step = sum(higher) if higher else jnp.int32(0)
            row = target - (level + step) * row_count
            column = sources[level, 0, slot] - me
            column = jnp.where(column < 0, column + cols, column)
            place = found[lists - 1]
            for j in range(lists - 1):
                place = jnp.where(step == j, found[j], place)
            plan[first_list + step, place] = (slot << (2 * field)) + (row << field) + column
            return tuple(found[j] + (step == j).astype(jnp.int32) for j in range(lists))

        found = lax.fori_loop(0, counts[level], one_slot, (jnp.int32(0),) * lists)
        for j in range(lists):
            plan[len(pairs), first_list + j] = found[j]
            for extra in range(slot_group):
                plan[first_list + j, found[j] + extra] = spare
    stage.wait()


def make_plan(row_count, cols, sources, targets, counts, blocks):
    width = -(-(sources.shape[-1] + slot_group) // 128) * 128
    return pl.pallas_call(
        functools.partial(plan_kernel, row_count, cols),
        out_shape=[
            jax.ShapeDtypeStruct((8, width), jnp.int32),
            pltpu.VMEM(blocks.shape[1:], blocks.dtype),
        ],
        in_specs=[hbm] * 4,
        out_specs=[smem, vmem],
        scratch_shapes=[
            pltpu.SMEM(sources.shape, jnp.int32),
            pltpu.SMEM(targets.shape, jnp.int32),
            pltpu.SMEM(counts.shape, jnp.int32),
            pltpu.SemaphoreType.DMA((4,)),
        ],
        compiler_params=params,
    )(in_hbm(sources), in_hbm(targets), in_hbm(counts), blocks)


def fetched_levels(lists, resident):
    needed = dict.fromkeys((layer, pairs[pair][0]) for pair, layer, _ in lists)
    return [key for key in needed if key != resident]


def update_kernel(config, *refs):
    lists, layer_count, groups_of_solutions, cols, row_count, resident, stages, carries = config
    refs = list(refs)
    plans_in = [refs.pop(0) for _ in range(layer_count)]
    blocks = [refs.pop(0) for _ in range(layer_count)]
    solutions = [refs.pop(0) for _ in range(groups_of_solutions * cols)]
    resident_ref = refs.pop(0) if resident else None
    total_in = refs.pop(0) if carries else None
    out = refs.pop(0)
    next_ref = refs.pop(0) if stages else None
    chosen, total, plans, plan_semaphores, semaphores = refs[:5]
    fetched = fetched_levels(lists, resident)

    plan_loads = [
        pltpu.make_async_copy(plans_in[n], plans.at[n], plan_semaphores.at[n])
        for n in range(layer_count)
    ]
    loads = {
        key: pltpu.make_async_copy(blocks[key[0]].at[key[1]], refs[5].at[k], semaphores.at[k])
        for k, key in enumerate(fetched)
    }
    for load in plan_loads + list(loads.values()):
        load.start()
    if stages:
        stage = pltpu.make_async_copy(blocks[0].at[stages], next_ref, semaphores.at[len(fetched)])
        stage.start()

    for j, solution_ref in enumerate(solutions):
        chosen[j] = solution_ref[...]
    if carries:
        total[:row_count] = total_in[...]
    else:
        total[...] = jnp.zeros_like(total)
    for load in plan_loads:
        load.wait()

    for pair, layer, j in lists:
        key = (layer, pairs[pair][0])
        if key in loads:
            loads.pop(key).wait()
        pieces = resident_ref if key == resident else refs[5].at[fetched.index(key)]

        def one_group(g, unused):
            for s in range(slot_group):
                entry = plans[layer, pair, g * slot_group + s]
                place = lax.shift_right_logical(entry, field) & field_mask
                column = j * cols + (entry & field_mask)
                total[place] += jnp.dot(
                    pieces[lax.shift_right_logical(entry, 2 * field)],
                    chosen[column],
                    preferred_element_type=jnp.float32,
                )
            return unused

        live = plans[layer, len(pairs), pair]
        lax.fori_loop(0, (live + slot_group - 1) // slot_group, one_group, 0)

    out[...] = total[:row_count].astype(out.dtype)
    if stages:
        stage.wait()


def update(
    lists, plans, blocks, solution_groups, total_in, row_count, sends, resident, resident_blocks, stages
):
    cols = len(solution_groups[0])
    width, sides = solution_groups[0][0].shape
    solutions = [part for group in solution_groups for part in group]
    operands = plans + blocks + solutions
    specs = [anywhere] * len(plans) + [hbm] * len(blocks) + [vmem] * len(solutions)
    for extra in (resident_blocks, total_in):
        if extra is not None:
            operands.append(extra)
            specs.append(vmem)
    fetched = fetched_levels(lists, resident)
    outs = [
        jax.ShapeDtypeStruct((row_count, width, sides), jnp.bfloat16 if sends else jnp.float32)
    ]
    if stages:
        outs.append(pltpu.VMEM(blocks[0].shape[1:], blocks[0].dtype))
    config = (
        lists, len(plans), len(solution_groups), cols, row_count, resident, stages,
        total_in is not None,
    )
    scratch = [
        pltpu.VMEM((len(solutions), width, sides), jnp.bfloat16),
        pltpu.VMEM((row_count + 1, width, sides), jnp.float32),
        pltpu.SMEM((len(plans),) + plans[0].shape, jnp.int32),
        pltpu.SemaphoreType.DMA((len(plans),)),
        pltpu.SemaphoreType.DMA((len(fetched) + 1,)),
    ]
    if fetched:
        scratch.append(pltpu.VMEM((len(fetched),) + blocks[0].shape[1:], jnp.bfloat16))
    found = pl.pallas_call(
        functools.partial(update_kernel, config),
        out_shape=outs,
        in_specs=specs,
        out_specs=[vmem] * len(outs),
        scratch_shapes=scratch,
        compiler_params=params,
    )(*operands)
    return found if stages else found[0]


def solve_block(inverse, residual):
    return jnp.dot(inverse, residual, preferred_element_type=jnp.float32).astype(jnp.bfloat16)


def reduced_solve(received, given, inverse):
    incoming = jnp.sum(received.astype(jnp.float32), axis=0)
    residual = (given.astype(jnp.float32) - incoming).astype(jnp.bfloat16)
    return solve_block(inverse, residual)


def exchange(send):
    return lax.all_to_all(send, "prow", 0, 0, tiled=True)


def local(blocks, sources, targets, counts, given_sub, given_top, inverse_sub, inverse_top):
    row_count = lax.axis_size("prow")
    cols = lax.axis_size("pcol")
    levels, capacity = sources.shape[3:]
    block_set = blocks[0, 0, 0]
    right_sub = given_sub[0, 0, 0]
    factor_sub = inverse_sub[0, 0, 0]
    right_top = given_top[0, 0]
    factor_top = inverse_top[0, 0]

    level_zero = solve_block(factor_sub[0], right_sub[0])
    zero_own = sibling_values(level_zero, 0)
    block_own = in_hbm(block_set)
    plan, staged = make_plan(
        row_count, cols,
        sources.reshape(levels, 1, capacity), targets.reshape(levels, 1, capacity),
        counts.reshape(levels), block_own,
    )
    both = [block_own, in_hbm(from_other_core(block_set))]

    send = update(
        [(0, 0, 0)], [plan], both[:1], [zero_own], None, row_count, True, (0, 0), staged, 0
    )
    send, zero_sent, plan_sent = lax.optimization_barrier((send, level_zero, plan))
    received = exchange(send)
    zero_other = sibling_values(zero_sent, 1)
    plans = [plan, from_other_core(plan_sent)]
    second, staged = update(
        [(1, 0, 0), (1, 1, 1)], plans, both, [zero_own, zero_other], None, row_count, False,
        None, None, 1,
    )
    received, second, staged = lax.optimization_barrier((received, second, staged))
    level_one = reduced_solve(received, right_sub[1], factor_sub[1])
    one_own = sibling_values(level_one, 0)
    one_other = sibling_values(level_one, 1)

    send = update(
        [(3, 0, 0), (3, 1, 1)], plans, both, [one_own, one_other], second, row_count, True,
        (0, 1), staged, 0,
    )
    received = exchange(send)
    third, staged = update(
        [(2, 0, 0), (2, 1, 1), (4, 0, 2), (4, 1, 3)], plans, both,
        [zero_own, zero_other, one_own, one_other], None, row_count, False, None, None, 2,
    )
    received, third, staged = lax.optimization_barrier((received, third, staged))
    level_two = reduced_solve(received, right_top[0], factor_top[0])
    two_own = sibling_values(level_two, 0)

    send = update(
        [(5, 0, 0), (5, 1, 0)], plans, both, [two_own], third, row_count, True, (0, 2), staged, 0
    )
    level_three = reduced_solve(exchange(send), right_top[1], factor_top[1])
    solved_sub = jnp.stack([level_zero, level_one])[None, None, None]
    solved_top = jnp.stack([level_two, level_three])[None, None]
    return (solved_sub, solved_top)


def solution(mesh):
    in_specs = (
        P("prow", "pcol", "zgrid", None, None, None, None),
        P("prow", "pcol", "zgrid", None, None),
        P("prow", "pcol", "zgrid", None, None),
        P("prow", "pcol", "zgrid", None),
        P("prow", "pcol", "zgrid", None, None, None),
        P("prow", "pcol", None, None, None),
        P("prow", "pcol", "zgrid", None, None, None),
        P("prow", "pcol", None, None, None),
    )
    out_specs = (P("prow", "pcol", "zgrid", None, None, None), P("prow", "pcol", None, None, None))
    return jax.shard_map(local, mesh=mesh, in_specs=in_specs, out_specs=out_specs, check_vma=False)
```

profile of v0, /device:TPU:0, one launch (start us, length us, event | category | flops | bytes accessed | tf_op | source)
XLA Modules:
  0.0 61.9 jit_solution(3276949251584444515)
XLA Ops:
  1.1 0.9 %convolution_convert_fusion.3.refs_2_.refs_4_ = bf16[128,128]{1,0:T(8,128)(2,1)S(1)} fusion(bf16[1,1,1,2,128,128]{5,4,3,2,1,0:T(8,128)(2,1)} %param.12, bf16[1,1,1,2,128,128]{5,4,3,2,1,0:T(8,128)(2,1)} %param.14), kind=kOutput, calls=%fused_computation.3 | convolution fusion | flops 4210688 | bytes 98304 | tf_op jit(solution)/shard_map/dot_general | solution.py:216
  2.0 2.6 %collective-permute-start = (bf16[128,128]{1,0:T(8,128)(2,1)S(1)}, bf16[128,128]{1,0:T(8,128)(2,1)S(1)}, u32[]{:S(2)}, u32[]{:S(2)}) collective-permute-start(bf16[128,128]{1,0:T(8,128)(2,1)S(1)} %convolution_convert_fusion.3.refs_2_.refs_4_), channel_id=1, source_target_pairs={{0,2},{1,3},{2,0},{3,1},{4,6},{5,7},{6,4},{7,5},{8,10},{9,11},{10,... | collective-permute-start | bytes 98312 | tf_op jit(solution)/shard_map/ppermute | solution.py:34
  4.6 2.3 %shard_map.95 = (s32[8,128]{1,0:T(8,128)S(1)}, bf16[40,128,128]{2,1,0:T(8,128)(2,1)S(1)}) custom-call(s32[3,1,40]{2,1,0:T(1,128)} %bitcast.81, s32[3,1,40]{2,1,0:T(1,128)} %bitcast.82, s32[3]{0:T(128)} %bitcast.83, bf16[3,40,128,128]{3,2,1,0:T(8,128)(2,1)} %bitcast.75), custom_call_target="tpu_custom_call" | custom-call | tf_op jit(solution)/shard_map/pallas_call | solution.py:88
  6.9 1.8 %shard_map.96 = bf16[8,128,128]{2,1,0:T(8,128)(2,1)} custom-call(s32[8,128]{1,0:T(8,128)S(1)} %get-tuple-element.20.refs_0_, bf16[3,40,128,128]{3,2,1,0:T(8,128)(2,1)} %bitcast.76, bf16[128,128]{1,0:T(8,128)(2,1)S(1)} %convolution_convert_fusion.3.refs_2_.refs_4_, bf16[128,128]{1,0:T(8,128)(2,1)S(1)} %collective-permute-done.refs_3_.refs_5_, ...), custom_call_target="tpu_custom_call" | custom-call | tf_op jit(solution)/shard_map/pallas_call | solution.py:204
  8.8 5.6 %all-to-all-start = ((bf16[8,128,128]{2,1,0:T(8,128)(2,1)}), bf16[8,128,128]{2,1,0:T(8,128)(2,1)S(1)}, u32[]{:S(2)}, u32[]{:S(2)}) async-start(bf16[8,128,128]{2,1,0:T(8,128)(2,1)} %shard_map.96), calls=%async_computation | async-start | bytes 524288 | tf_op jit(solution)/shard_map/all_to_all | solution.py:226
  14.5 1.6 %collective-permute-start.3 = (bf16[128,128]{1,0:T(8,128)(2,1)S(1)}, bf16[128,128]{1,0:T(8,128)(2,1)S(1)}, u32[]{:S(2)}, u32[]{:S(2)}) collective-permute-start(bf16[128,128]{1,0:T(8,128)(2,1)S(1)} %convolution_convert_fusion.3.refs_2_.refs_4_), channel_id=1, source_target_pairs={{0,1},{1,0},{2,3},{3,2},{4,5},{5,4},{6,7},{7,6},{8,9},{9,8},{10,11... | collective-permute-start | bytes 98312 | tf_op jit(solution)/shard_map/ppermute | solution.py:34
  16.1 1.2 %collective-permute-done.1.refs_1_ = s32[8,128]{1,0:T(8,128)S(1)} collective-permute-done((s32[8,128]{1,0:T(8,128)S(1)}, s32[8,128]{1,0:T(8,128)S(1)}, u32[]{:S(2)}, u32[]{:S(2)}) %collective-permute-start.1) | collective-permute-done | bytes 4128 | tf_op jit(solution)/shard_map/ppermute | solution.py:39
  17.3 0.8 %collective-permute-done.4.refs_7_ = bf16[128,128]{1,0:T(8,128)(2,1)S(1)} collective-permute-done((bf16[128,128]{1,0:T(8,128)(2,1)S(1)}, bf16[128,128]{1,0:T(8,128)(2,1)S(1)}, u32[]{:S(2)}, u32[]{:S(2)}) %collective-permute-start.4) | collective-permute-done | bytes 32800 | tf_op jit(solution)/shard_map/ppermute | solution.py:34
  18.1 2.3 %shard_map.97 = (f32[8,128,128]{2,1,0:T(8,128)S(1)}, bf16[40,128,128]{2,1,0:T(8,128)(2,1)S(1)}) custom-call(s32[8,128]{1,0:T(8,128)S(1)} %get-tuple-element.20.refs_0_, s32[8,128]{1,0:T(8,128)S(1)} %collective-permute-done.1.refs_1_, bf16[3,40,128,128]{3,2,1,0:T(8,128)(2,1)} %bitcast.77, bf16[3,40,128,128]{3,2,1,0:T(8,128)(2,1)} %collective-permute-done.2.refs_3_, ...), custom_call_target="tpu_custom_call" | custom-call | tf_op jit(solution)/shard_map/pallas_call | solution.py:204
  20.5 2.9 %all-to-all-done = bf16[8,128,128]{2,1,0:T(8,128)(2,1)S(1)} async-done(((bf16[8,128,128]{2,1,0:T(8,128)(2,1)}), bf16[8,128,128]{2,1,0:T(8,128)(2,1)S(1)}, u32[]{:S(2)}, u32[]{:S(2)}) %all-to-all-start) | async-done | bytes 262176 | tf_op jit(solution)/shard_map/all_to_all | solution.py:226
  23.6 1.0 %collective-permute-start.6 = (bf16[128,128]{1,0:T(8,128)(2,1)S(1)}, bf16[128,128]{1,0:T(8,128)(2,1)S(1)}, u32[]{:S(2)}, u32[]{:S(2)}) collective-permute-start(bf16[128,128]{1,0:T(8,128)(2,1)S(1)} %bitcast.66), channel_id=1, source_target_pairs={{0,1},{1,0},{2,3},{3,2},{4,5},{5,4},{6,7},{7,6},{8,9},{9,8},{10,11... | collective-permute-start | bytes 98312 | tf_op jit(solution)/shard_map/ppermute | solution.py:34
  24.6 1.1 %collective-permute-start.5 = (bf16[128,128]{1,0:T(8,128)(2,1)S(1)}, bf16[128,128]{1,0:T(8,128)(2,1)S(1)}, u32[]{:S(2)}, u32[]{:S(2)}) collective-permute-start(bf16[128,128]{1,0:T(8,128)(2,1)S(1)} %bitcast.67), channel_id=1, source_target_pairs={{0,2},{1,3},{2,0},{3,1},{4,6},{5,7},{6,4},{7,5},{8,10},{9,11},{10,... | collective-permute-start | bytes 98312 | tf_op jit(solution)/shard_map/ppermute | solution.py:34
  25.7 1.2 %collective-permute-done.7.refs_7_.refs_11_ = bf16[128,128]{1,0:T(8,128)(2,1)S(1)} collective-permute-done((bf16[128,128]{1,0:T(8,128)(2,1)S(1)}, bf16[128,128]{1,0:T(8,128)(2,1)S(1)}, u32[]{:S(2)}, u32[]{:S(2)}) %collective-permute-start.7) | collective-permute-done | bytes 32800 | tf_op jit(solution)/shard_map/ppermute | solution.py:34
  26.9 1.6 %collective-permute-done.5.refs_5_.refs_9_ = bf16[128,128]{1,0:T(8,128)(2,1)S(1)} collective-permute-done((bf16[128,128]{1,0:T(8,128)(2,1)S(1)}, bf16[128,128]{1,0:T(8,128)(2,1)S(1)}, u32[]{:S(2)}, u32[]{:S(2)}) %collective-permute-start.5) | collective-permute-done | bytes 32800 | tf_op jit(solution)/shard_map/ppermute | solution.py:34
  28.5 2.8 %shard_map.98 = bf16[8,128,128]{2,1,0:T(8,128)(2,1)} custom-call(s32[8,128]{1,0:T(8,128)S(1)} %get-tuple-element.20.refs_0_, s32[8,128]{1,0:T(8,128)S(1)} %collective-permute-done.1.refs_1_, bf16[3,40,128,128]{3,2,1,0:T(8,128)(2,1)} %bitcast.78, bf16[3,40,128,128]{3,2,1,0:T(8,128)(2,1)} %collective-permute-done.2.refs_3_, bf16[128,128]{1,0:T(8,128)(2,1)S(1)} %bitcast.68, ...), custom_call_target="tpu_custom_call" | custom-call | tf_op jit(solution)/shard_map/pallas_call | solution.py:204
  31.3 3.4 %all-to-all-start.1 = ((bf16[8,128,128]{2,1,0:T(8,128)(2,1)}), bf16[8,128,128]{2,1,0:T(8,128)(2,1)S(1)}, u32[]{:S(2)}, u32[]{:S(2)}) async-start(bf16[8,128,128]{2,1,0:T(8,128)(2,1)} %shard_map.98), calls=%async_computation.1 | async-start | bytes 524288 | tf_op jit(solution)/shard_map/all_to_all | solution.py:226
  34.7 3.1 %shard_map.99 = (f32[8,128,128]{2,1,0:T(8,128)S(1)}, bf16[40,128,128]{2,1,0:T(8,128)(2,1)S(1)}) custom-call(s32[8,128]{1,0:T(8,128)S(1)} %get-tuple-element.20.refs_0_, s32[8,128]{1,0:T(8,128)S(1)} %collective-permute-done.1.refs_1_, bf16[3,40,128,128]{3,2,1,0:T(8,128)(2,1)} %bitcast.79, bf16[3,40,128,128]{3,2,1,0:T(8,128)(2,1)} %collective-permute-done.2.refs_3_, ...), custom_call_target="tpu_custom_call" | custom-call | tf_op jit(solution)/shard_map/pallas_call | solution.py:204
  37.8 5.0 %all-to-all-done.1 = bf16[8,128,128]{2,1,0:T(8,128)(2,1)S(1)} async-done(((bf16[8,128,128]{2,1,0:T(8,128)(2,1)}), bf16[8,128,128]{2,1,0:T(8,128)(2,1)S(1)}, u32[]{:S(2)}, u32[]{:S(2)}) %all-to-all-start.1) | async-done | bytes 262176 | tf_op jit(solution)/shard_map/all_to_all | solution.py:226
  43.0 0.9 %collective-permute-start.8 = (bf16[128,128]{1,0:T(8,128)(2,1)S(1)}, bf16[128,128]{1,0:T(8,128)(2,1)S(1)}, u32[]{:S(2)}, u32[]{:S(2)}) collective-permute-start(bf16[128,128]{1,0:T(8,128)(2,1)S(1)} %bitcast.71), channel_id=1, source_target_pairs={{0,2},{1,3},{2,0},{3,1},{4,6},{5,7},{6,4},{7,5},{8,10},{9,11},{10,... | collective-permute-start | bytes 98312 | tf_op jit(solution)/shard_map/ppermute | solution.py:34
  43.9 3.0 %collective-permute-done.8.refs_5_ = bf16[128,128]{1,0:T(8,128)(2,1)S(1)} collective-permute-done((bf16[128,128]{1,0:T(8,128)(2,1)S(1)}, bf16[128,128]{1,0:T(8,128)(2,1)S(1)}, u32[]{:S(2)}, u32[]{:S(2)}) %collective-permute-start.8) | collective-permute-done | bytes 32800 | tf_op jit(solution)/shard_map/ppermute | solution.py:34
  47.0 2.5 %shard_map.100 = bf16[8,128,128]{2,1,0:T(8,128)(2,1)} custom-call(s32[8,128]{1,0:T(8,128)S(1)} %get-tuple-element.20.refs_0_, s32[8,128]{1,0:T(8,128)S(1)} %collective-permute-done.1.refs_1_, bf16[3,40,128,128]{3,2,1,0:T(8,128)(2,1)} %bitcast.80, bf16[3,40,128,128]{3,2,1,0:T(8,128)(2,1)} %collective-permute-done.2.refs_3_, bf16[128,128]{1,0:T(8,128)(2,1)S(1)} %bitcast.72, ...), custom_call_target="tpu_custom_call" | custom-call | tf_op jit(solution)/shard_map/pallas_call | solution.py:204
  49.5 3.4 %all-to-all-start.2 = ((bf16[8,128,128]{2,1,0:T(8,128)(2,1)}), bf16[8,128,128]{2,1,0:T(8,128)(2,1)S(1)}, u32[]{:S(2)}, u32[]{:S(2)}) async-start(bf16[8,128,128]{2,1,0:T(8,128)(2,1)} %shard_map.100), calls=%async_computation.2 | async-start | bytes 524288 | tf_op jit(solution)/shard_map/all_to_all | solution.py:226
  53.6 7.5 %all-to-all-done.2 = bf16[8,128,128]{2,1,0:T(8,128)(2,1)S(1)} async-done(((bf16[8,128,128]{2,1,0:T(8,128)(2,1)}), bf16[8,128,128]{2,1,0:T(8,128)(2,1)S(1)}, u32[]{:S(2)}, u32[]{:S(2)}) %all-to-all-start.2) | async-done | bytes 262176 | tf_op jit(solution)/shard_map/all_to_all | solution.py:226
  61.3 0.6 %maximum_bitcast_fusion.1 = bf16[1,1,2,128,128]{4,3,2,1,0:T(8,128)(2,1)} fusion(bf16[1,128,128]{2,1,0:T(8,128)(2,1)S(1)} %fusion, bf16[1,128,128]{2,1,0:T(8,128)(2,1)S(1)} %bitcast.73), kind=kLoop, calls=%fused_computation.9 | loop fusion | flops 32768 | bytes 131072 | tf_op jit(solution)/shard_map/broadcast_in_dim | solution.py:283
  (23 shorter events, 1.8 us)
Async XLA Ops:
  0.6 17.5 %collective-permute-start.2 = (bf16[3,40,128,128]{3,2,1,0:T(8,128)(2,1)}, bf16[3,40,128,128]{3,2,1,0:T(8,128)(2,1)}, u32[]{:S(2)}, u32[]{:S(2)}) collective-permute-start(bf16[3,40,128,128]{3,2,1,0:T(8,128)(2,1)} %bitcast.74), channel_id=1, source_target_pairs={{0,1},{1,0},{2,3},{3,2},{4,5},{5,4},{6,7},{7,6},{8,9},{9,8},{10,11... | collective-permute-start | bytes 11796488 | tf_op jit(solution)/shard_map/ppermute | solution.py:39
  2.0 4.9 %collective-permute-start = (bf16[128,128]{1,0:T(8,128)(2,1)S(1)}, bf16[128,128]{1,0:T(8,128)(2,1)S(1)}, u32[]{:S(2)}, u32[]{:S(2)}) collective-permute-start(bf16[128,128]{1,0:T(8,128)(2,1)S(1)} %convolution_convert_fusion.3.refs_2_.refs_4_), channel_id=1, source_target_pairs={{0,2},{1,3},{2,0},{3,1},{4,6},{5,7},{6,4},{7,5},{8,10},{9,11},{10,... | collective-permute-start | bytes 98312 | tf_op jit(solution)/shard_map/ppermute | solution.py:34
  8.8 14.6 %all-to-all-start = ((bf16[8,128,128]{2,1,0:T(8,128)(2,1)}), bf16[8,128,128]{2,1,0:T(8,128)(2,1)S(1)}, u32[]{:S(2)}, u32[]{:S(2)}) async-start(bf16[8,128,128]{2,1,0:T(8,128)(2,1)} %shard_map.96), calls=%async_computation | async-start | bytes 524288 | tf_op jit(solution)/shard_map/all_to_all | solution.py:226
  14.4 9.0 %copy-start = (bf16[1,1,1,2,128,128]{5,4,3,2,1,0:T(8,128)(2,1)S(1)}, bf16[1,1,1,2,128,128]{5,4,3,2,1,0:T(8,128)(2,1)}, u32[]{:S(2)}) copy-start(bf16[1,1,1,2,128,128]{5,4,3,2,1,0:T(8,128)(2,1)} %param.12) | copy-start | bytes 196612
  14.4 9.0 %copy-start.1 = (bf16[1,1,1,2,128,128]{5,4,3,2,1,0:T(8,128)(2,1)S(1)}, bf16[1,1,1,2,128,128]{5,4,3,2,1,0:T(8,128)(2,1)}, u32[]{:S(2)}) copy-start(bf16[1,1,1,2,128,128]{5,4,3,2,1,0:T(8,128)(2,1)} %param.14) | copy-start | bytes 196612
  14.4 3.7 %collective-permute-start.4 = (bf16[128,128]{1,0:T(8,128)(2,1)S(1)}, bf16[128,128]{1,0:T(8,128)(2,1)S(1)}, u32[]{:S(2)}, u32[]{:S(2)}) collective-permute-start(bf16[128,128]{1,0:T(8,128)(2,1)S(1)} %convolution_convert_fusion.3.refs_2_.refs_4_), channel_id=1, source_target_pairs={{0,3},{1,2},{2,1},{3,0},{4,7},{5,6},{6,5},{7,4},{8,11},{9,10},{10,... | collective-permute-start | bytes 98312 | tf_op jit(solution)/shard_map/ppermute | solution.py:34
  14.5 3.6 %collective-permute-start.3 = (bf16[128,128]{1,0:T(8,128)(2,1)S(1)}, bf16[128,128]{1,0:T(8,128)(2,1)S(1)}, u32[]{:S(2)}, u32[]{:S(2)}) collective-permute-start(bf16[128,128]{1,0:T(8,128)(2,1)S(1)} %convolution_convert_fusion.3.refs_2_.refs_4_), channel_id=1, source_target_pairs={{0,1},{1,0},{2,3},{3,2},{4,5},{5,4},{6,7},{7,6},{8,9},{9,8},{10,11... | collective-permute-start | bytes 98312 | tf_op jit(solution)/shard_map/ppermute | solution.py:34
  16.1 1.2 %collective-permute-start.1 = (s32[8,128]{1,0:T(8,128)S(1)}, s32[8,128]{1,0:T(8,128)S(1)}, u32[]{:S(2)}, u32[]{:S(2)}) collective-permute-start(s32[8,128]{1,0:T(8,128)S(1)} %get-tuple-element.20.refs_0_), channel_id=1, source_target_pairs={{0,1},{1,0},{2,3},{3,2},{4,5},{5,4},{6,7},{7,6},{8,9},{9,8},{10,11... | collective-permute-start | bytes 12296 | tf_op jit(solution)/shard_map/ppermute | solution.py:39
  23.5 3.4 %collective-permute-start.7 = (bf16[128,128]{1,0:T(8,128)(2,1)S(1)}, bf16[128,128]{1,0:T(8,128)(2,1)S(1)}, u32[]{:S(2)}, u32[]{:S(2)}) collective-permute-start(bf16[128,128]{1,0:T(8,128)(2,1)S(1)} %bitcast.65), channel_id=1, source_target_pairs={{0,3},{1,2},{2,1},{3,0},{4,7},{5,6},{6,5},{7,4},{8,11},{9,10},{10,... | collective-permute-start | bytes 98312 | tf_op jit(solution)/shard_map/ppermute | solution.py:34
  23.6 3.3 %collective-permute-start.6 = (bf16[128,128]{1,0:T(8,128)(2,1)S(1)}, bf16[128,128]{1,0:T(8,128)(2,1)S(1)}, u32[]{:S(2)}, u32[]{:S(2)}) collective-permute-start(bf16[128,128]{1,0:T(8,128)(2,1)S(1)} %bitcast.66), channel_id=1, source_target_pairs={{0,1},{1,0},{2,3},{3,2},{4,5},{5,4},{6,7},{7,6},{8,9},{9,8},{10,11... | collective-permute-start | bytes 98312 | tf_op jit(solution)/shard_map/ppermute | solution.py:34
  24.6 3.9 %collective-permute-start.5 = (bf16[128,128]{1,0:T(8,128)(2,1)S(1)}, bf16[128,128]{1,0:T(8,128)(2,1)S(1)}, u32[]{:S(2)}, u32[]{:S(2)}) collective-permute-start(bf16[128,128]{1,0:T(8,128)(2,1)S(1)} %bitcast.67), channel_id=1, source_target_pairs={{0,2},{1,3},{2,0},{3,1},{4,6},{5,7},{6,4},{7,5},{8,10},{9,11},{10,... | collective-permute-start | bytes 98312 | tf_op jit(solution)/shard_map/ppermute | solution.py:34
  31.3 11.6 %all-to-all-start.1 = ((bf16[8,128,128]{2,1,0:T(8,128)(2,1)}), bf16[8,128,128]{2,1,0:T(8,128)(2,1)S(1)}, u32[]{:S(2)}, u32[]{:S(2)}) async-start(bf16[8,128,128]{2,1,0:T(8,128)(2,1)} %shard_map.98), calls=%async_computation.1 | async-start | bytes 524288 | tf_op jit(solution)/shard_map/all_to_all | solution.py:226
  34.7 8.2 %copy-start.2 = (bf16[1,1,2,128,128]{4,3,2,1,0:T(8,128)(2,1)S(1)}, bf16[1,1,2,128,128]{4,3,2,1,0:T(8,128)(2,1)}, u32[]{:S(2)}) copy-start(bf16[1,1,2,128,128]{4,3,2,1,0:T(8,128)(2,1)} %param.15) | copy-start | bytes 196612
  34.7 8.2 %copy-start.3 = (bf16[1,1,2,128,128]{4,3,2,1,0:T(8,128)(2,1)S(1)}, bf16[1,1,2,128,128]{4,3,2,1,0:T(8,128)(2,1)}, u32[]{:S(2)}) copy-start(bf16[1,1,2,128,128]{4,3,2,1,0:T(8,128)(2,1)} %param.13) | copy-start | bytes 196612
  43.0 3.9 %collective-permute-start.8 = (bf16[128,128]{1,0:T(8,128)(2,1)S(1)}, bf16[128,128]{1,0:T(8,128)(2,1)S(1)}, u32[]{:S(2)}, u32[]{:S(2)}) collective-permute-start(bf16[128,128]{1,0:T(8,128)(2,1)S(1)} %bitcast.71), channel_id=1, source_target_pairs={{0,2},{1,3},{2,0},{3,1},{4,6},{5,7},{6,4},{7,5},{8,10},{9,11},{10,... | collective-permute-start | bytes 98312 | tf_op jit(solution)/shard_map/ppermute | solution.py:34
  49.5 11.6 %all-to-all-start.2 = ((bf16[8,128,128]{2,1,0:T(8,128)(2,1)}), bf16[8,128,128]{2,1,0:T(8,128)(2,1)S(1)}, u32[]{:S(2)}, u32[]{:S(2)}) async-start(bf16[8,128,128]{2,1,0:T(8,128)(2,1)} %shard_map.100), calls=%async_computation.2 | async-start | bytes 524288 | tf_op jit(solution)/shard_map/all_to_all | solution.py:226
where the time goes:
time: 62.8 us; the launch traced here: 61.9 us
  waiting for transfers between devices  23.3 us (37%)
  starting transfers between devices  20.3 us (32%)
  Pallas kernels  14.9 us (24%)
  other arithmetic  1.4 us (2%)
  matrix products  1.3 us (2%)
  between operations  0.79 us (1%)
    all_to_all x3, waiting for transfers between devices, exchange(): return lax.all_to_all(send, 'prow', 0, 0, tiled=True)  15.4 us
    pallas_call x5, Pallas kernels, update(): pl.pallas_call(functools.partial(update_kernel, config), out_shape=outs,...  12.5 us
    all_to_all x3, starting transfers between devices, exchange(): return lax.all_to_all(send, 'prow', 0, 0, tiled=True)  12.5 us
    ppermute x7, starting transfers between devices, sibling_values(): found.append(lax.ppermute(value, ('pcol', 'zgrid'), moves))  7.29 us
    ppermute x7, waiting for transfers between devices, sibling_values(): found.append(lax.ppermute(value, ('pcol', 'zgrid'), moves))  6.64 us
    pallas_call x1, Pallas kernels, make_plan(): pl.pallas_call(functools.partial(plan_kernel, row_count, cols), out_shape...  2.32 us
    dot_general x4, matrix products, solve_block(): jnp.dot(inverse, residual, preferred_element_type=jnp.float32)  1.3 us
  transfers between devices with their start and end apart: 12, of which 8 were waited for; matrix products, arithmetic and copies ran while one was open for 2% of the time, Pallas kernels for 15%

commit v1 on v0

--- a/solution.py
+++ b/solution.py
@@ -57,27 +57,32 @@
     for load in loads:
         load.wait()
     me = lax.axis_index("pcol")
-    spare = row_count << field
+    my_parity = lax.axis_index("prow") & 1
+    spare = (row_count // 2) << field
+    list_count = 2 * len(pairs)
     for level in range(3):
-        first_list = pairs.index((level, level + 1))
-        lists = 3 - level
+        first_list = 2 * pairs.index((level, level + 1))
+        steps = 3 - level
+        lists = 2 * steps
 
         def one_slot(slot, found):
             target = targets[level, 0, slot]
-            higher = [(target >= (level + j) * row_count).astype(jnp.int32) for j in range(1, lists)]
+            higher = [(target >= (level + j) * row_count).astype(jnp.int32) for j in range(1, steps)]
             step = sum(higher) if higher else jnp.int32(0)
             row = target - (level + step) * row_count
+            kind = 2 * step + ((row & 1) ^ my_parity)
             column = sources[level, 0, slot] - me
             column = jnp.where(column < 0, column + cols, column)
             place = found[lists - 1]
             for j in range(lists - 1):
-                place = jnp.where(step == j, found[j], place)
-            plan[first_list + step, place] = (slot << (2 * field)) + (row << field) + column
-            return tuple(found[j] + (step == j).astype(jnp.int32) for j in range(lists))
+                place = jnp.where(kind == j, found[j], place)
+            half_row = lax.shift_right_logical(row, 1)
+            plan[first_list + kind, place] = (slot << (2 * field)) + (half_row << field) + column
+            return tuple(found[j] + (kind == j).astype(jnp.int32) for j in range(lists))
 
         found = lax.fori_loop(0, counts[level], one_slot, (jnp.int32(0),) * lists)
         for j in range(lists):
-            plan[len(pairs), first_list + j] = found[j]
+            plan[list_count, first_list + j] = found[j]
             for extra in range(slot_group):
                 plan[first_list + j, found[j] + extra] = spare
     stage.wait()
@@ -88,7 +93,7 @@
     return pl.pallas_call(
         functools.partial(plan_kernel, row_count, cols),
         out_shape=[
-            jax.ShapeDtypeStruct((8, width), jnp.int32),
+            jax.ShapeDtypeStruct((16, width), jnp.int32),
             pltpu.VMEM(blocks.shape[1:], blocks.dtype),
         ],
         in_specs=[hbm] * 4,
@@ -109,7 +114,7 @@
 
 
 def update_kernel(config, *refs):
-    lists, layer_count, groups_of_solutions, cols, row_count, resident, stages, carries = config
+    lists, parities, layer_count, groups_of_solutions, cols, half_rows, resident, stages, carries = config
     refs = list(refs)
     plans_in = [refs.pop(0) for _ in range(layer_count)]
     blocks = [refs.pop(0) for _ in range(layer_count)]
@@ -138,7 +143,8 @@
     for j, solution_ref in enumerate(solutions):
         chosen[j] = solution_ref[...]
     if carries:
-        total[:row_count] = total_in[...]
+        for n, parity in enumerate(parities):
+            total[n, :half_rows] = total_in[parity]
     else:
         total[...] = jnp.zeros_like(total)
     for load in plan_loads:
@@ -150,28 +156,33 @@
             loads.pop(key).wait()
         pieces = resident_ref if key == resident else refs[5].at[fetched.index(key)]
 
-        def one_group(g, unused):
-            for s in range(slot_group):
-                entry = plans[layer, pair, g * slot_group + s]
-                place = lax.shift_right_logical(entry, field) & field_mask
-                column = j * cols + (entry & field_mask)
-                total[place] += jnp.dot(
-                    pieces[lax.shift_right_logical(entry, 2 * field)],
-                    chosen[column],
-                    preferred_element_type=jnp.float32,
-                )
-            return unused
-
-        live = plans[layer, len(pairs), pair]
-        lax.fori_loop(0, (live + slot_group - 1) // slot_group, one_group, 0)
-
-    out[...] = total[:row_count].astype(out.dtype)
+        for n, parity in enumerate(parities):
+            which = 2 * pair + parity
+
+            def one_group(g, unused):
+                for s in range(slot_group):
+                    entry = plans[layer, which, g * slot_group + s]
+                    place = lax.shift_right_logical(entry, field) & field_mask
+                    column = j * cols + (entry & field_mask)
+                    total[n, place] += jnp.dot(
+                        pieces[lax.shift_right_logical(entry, 2 * field)],
+                        chosen[column],
+                        preferred_element_type=jnp.float32,
+                    )
+                return unused
+
+            live = plans[layer, 2 * len(pairs), which]
+            lax.fori_loop(0, (live + slot_group - 1) // slot_group, one_group, 0)
+
+    for n in range(len(parities)):
+        out[n] = total[n, :half_rows].astype(out.dtype)
     if stages:
         stage.wait()
 
 
 def update(
-    lists, plans, blocks, solution_groups, total_in, row_count, sends, resident, resident_blocks, stages
+    lists, parities, plans, blocks, solution_groups, total_in, half_rows, kind, resident,
+    resident_blocks, stages,
 ):
     cols = len(solution_groups[0])
     width, sides = solution_groups[0][0].shape
@@ -184,17 +195,17 @@
             specs.append(vmem)
     fetched = fetched_levels(lists, resident)
     outs = [
-        jax.ShapeDtypeStruct((row_count, width, sides), jnp.bfloat16 if sends else jnp.float32)
+        jax.ShapeDtypeStruct((len(parities), half_rows, width, sides), kind)
     ]
     if stages:
         outs.append(pltpu.VMEM(blocks[0].shape[1:], blocks[0].dtype))
     config = (
-        lists, len(plans), len(solution_groups), cols, row_count, resident, stages,
+        lists, parities, len(plans), len(solution_groups), cols, half_rows, resident, stages,
         total_in is not None,
     )
     scratch = [
         pltpu.VMEM((len(solutions), width, sides), jnp.bfloat16),
-        pltpu.VMEM((row_count + 1, width, sides), jnp.float32),
+        pltpu.VMEM((len(parities), half_rows + 1, width, sides), jnp.float32),
         pltpu.SMEM((len(plans),) + plans[0].shape, jnp.int32),
         pltpu.SemaphoreType.DMA((len(plans),)),
         pltpu.SemaphoreType.DMA((len(fetched) + 1,)),
@@ -222,8 +233,19 @@
     return solve_block(inverse, residual)
 
 
+def to_neighbour(value):
+    rows = lax.axis_size("prow")
+    return lax.ppermute(value, "prow", [(row, row ^ 1) for row in range(rows)])
+
+
+def pair_sum(own, received):
+    return (own[0] + received[0].astype(jnp.float32)).astype(jnp.bfloat16)
+
+
 def exchange(send):
-    return lax.all_to_all(send, "prow", 0, 0, tiled=True)
+    rows = lax.axis_size("prow")
+    groups = [list(range(parity, rows, 2)) for parity in range(2)]
+    return lax.all_to_all(send, "prow", 0, 0, tiled=True, axis_index_groups=groups)
 
 
 def local(blocks, sources, targets, counts, given_sub, given_top, inverse_sub, inverse_top):
@@ -246,38 +268,47 @@
     )
     both = [block_own, in_hbm(from_other_core(block_set))]
 
-    send = update(
-        [(0, 0, 0)], [plan], both[:1], [zero_own], None, row_count, True, (0, 0), staged, 0
-    )
+    half_rows = row_count // 2
+
+    def partials(lists, plans, blocks, solutions, total, resident, staged):
+        send = update(
+            lists, (1,), plans, blocks, solutions, total, half_rows, jnp.bfloat16, resident, staged, 0
+        )
+        received = to_neighbour(send)
+        own = update(
+            lists, (0,), plans, blocks, solutions, total, half_rows, jnp.float32, resident, staged, 0
+        )
+        received, own = lax.optimization_barrier((received, own))
+        return pair_sum(own, received)
+
+    send = partials([(0, 0, 0)], [plan], both[:1], [zero_own], None, (0, 0), staged)
     send, zero_sent, plan_sent = lax.optimization_barrier((send, level_zero, plan))
     received = exchange(send)
     zero_other = sibling_values(zero_sent, 1)
     plans = [plan, from_other_core(plan_sent)]
     second, staged = update(
-        [(1, 0, 0), (1, 1, 1)], plans, both, [zero_own, zero_other], None, row_count, False,
-        None, None, 1,
+        [(1, 0, 0), (1, 1, 1)], (0, 1), plans, both, [zero_own, zero_other], None, half_rows,
+        jnp.float32, None, None, 1,
     )
     received, second, staged = lax.optimization_barrier((received, second, staged))
     level_one = reduced_solve(received, right_sub[1], factor_sub[1])
     one_own = sibling_values(level_one, 0)
     one_other = sibling_values(level_one, 1)
 
-    send = update(
-        [(3, 0, 0), (3, 1, 1)], plans, both, [one_own, one_other], second, row_count, True,
-        (0, 1), staged, 0,
-    )
+    send = partials(
+        [(3, 0, 0), (3, 1, 1)], plans, both, [one_own, one_other], second, (0, 1), staged
+    )
+    send, one_own, one_other = lax.optimization_barrier((send, one_own, one_other))
     received = exchange(send)
     third, staged = update(
-        [(2, 0, 0), (2, 1, 1), (4, 0, 2), (4, 1, 3)], plans, both,
-        [zero_own, zero_other, one_own, one_other], None, row_count, False, None, None, 2,
+        [(2, 0, 0), (2, 1, 1), (4, 0, 2), (4, 1, 3)], (0, 1), plans, both,
+        [zero_own, zero_other, one_own, one_other], None, half_rows, jnp.float32, None, None, 2,
     )
     received, third, staged = lax.optimization_barrier((received, third, staged))
     level_two = reduced_solve(received, right_top[0], factor_top[0])
     two_own = sibling_values(level_two, 0)
 
-    send = update(
-        [(5, 0, 0), (5, 1, 0)], plans, both, [two_own], third, row_count, True, (0, 2), staged, 0
-    )
+    send = partials([(5, 0, 0), (5, 1, 0)], plans, both, [two_own], third, (0, 2), staged)
     level_three = reduced_solve(exchange(send), right_top[1], factor_top[1])
     solved_sub = jnp.stack([level_zero, level_one])[None, None, None]
     solved_top = jnp.stack([level_two, level_three])[None, None]

time: 62.8 us -> 71 us (1.13)
  starting transfers between devices: 20.3 us -> 26.6 us
  other arithmetic: 1.4 us -> 3.41 us
  waiting for transfers between devices: 23.3 us -> 21.6 us
  Pallas kernels: 14.9 us -> 16.4 us
    all_to_all x3, waiting for transfers between devices: 15.4 us -> 7.91 us  [exchange(): lax.all_to_all(send, 'prow', 0, 0, tiled=True, axis_index_groups=groups)]
    ppermute x0 -> x3, waiting for transfers between devices: none -> 6.25 us  [to_neighbour(): return lax.ppermute(value, 'prow', [(row, row ^ 1) for row in range(rows)])]
    ppermute x0 -> x3, starting transfers between devices: none -> 6.22 us  [to_neighbour(): return lax.ppermute(value, 'prow', [(row, row ^ 1) for row in range(rows)])]
    convert_element_type x0 -> x3, other arithmetic: none -> 2.06 us  [pair_sum(): return (own[0] + received[0].astype(jnp.float32)).astype(jnp.bfloat16)]
    pallas_call x5 -> x8, Pallas kernels: 12.5 us -> 13.8 us  [update(): pl.pallas_call(functools.partial(update_kernel, config), out_shape=outs,...]
  transfers between devices with their start and end apart: 12 -> 15, of which waited for: 8 -> 11; matrix products, arithmetic and copies ran while one was open for 2% -> 3% of each run, Pallas kernels for 15% -> 19%
where the time goes in v1:
time: 71 us; the launch traced here: 70.1 us
  starting transfers between devices  26.6 us (37%)
  waiting for transfers between devices  21.6 us (30%)
  Pallas kernels  16.4 us (23%)
  other arithmetic  3.41 us (5%)
  matrix products  1.29 us (2%)
  between operations  0.78 us (1%)
    pallas_call x8, Pallas kernels, update(): pl.pallas_call(functools.partial(update_kernel, config), out_shape=outs,...  13.8 us
    all_to_all x3, starting transfers between devices, exchange(): lax.all_to_all(send, 'prow', 0, 0, tiled=True, axis_index_groups=groups)  13.1 us
    all_to_all x3, waiting for transfers between devices, exchange(): lax.all_to_all(send, 'prow', 0, 0, tiled=True, axis_index_groups=groups)  7.91 us
    ppermute x7, starting transfers between devices, sibling_values(): found.append(lax.ppermute(value, ('pcol', 'zgrid'), moves))  6.64 us
    ppermute x7, waiting for transfers between devices, sibling_values(): found.append(lax.ppermute(value, ('pcol', 'zgrid'), moves))  6.38 us
    ppermute x3, waiting for transfers between devices, to_neighbour(): return lax.ppermute(value, 'prow', [(row, row ^ 1) for row in range(rows)])  6.25 us
    ppermute x3, starting transfers between devices, to_neighbour(): return lax.ppermute(value, 'prow', [(row, row ^ 1) for row in range(rows)])  6.22 us
    pallas_call x1, Pallas kernels, make_plan(): pl.pallas_call(functools.partial(plan_kernel, row_count, cols), out_shape...  2.57 us
  transfers between devices with their start and end apart: 15, of which 11 were waited for; matrix products, arithmetic and copies ran while one was open for 3% of the time, Pallas kernels for 19%

profile of v1, /device:TPU:0, one launch (start us, length us, event | category | flops | bytes accessed | tf_op | source)
XLA Modules:
  0.0 70.1 jit_solution(13364388348105887058)
XLA Ops:
  2.0 2.6 %collective-permute-start = (bf16[128,128]{1,0:T(8,128)(2,1)S(1)}, bf16[128,128]{1,0:T(8,128)(2,1)S(1)}, u32[]{:S(2)}, u32[]{:S(2)}) collective-permute-start(bf16[128,128]{1,0:T(8,128)(2,1)S(1)} %convolution_convert_fusion.3.refs_2_.refs_4_), channel_id=1, source_target_pairs={{0,2},{1,3},{2,0},{3,1},{4,6},{5,7},{6,4},{7,5},{8,10},{9,11},{10,... | collective-permute-start | bytes 98312 | tf_op jit(solution)/shard_map/ppermute | solution.py:34
  4.6 2.6 %shard_map.95 = (s32[16,128]{1,0:T(8,128)S(1)}, bf16[40,128,128]{2,1,0:T(8,128)(2,1)S(1)}) custom-call(s32[3,1,40]{2,1,0:T(1,128)} %bitcast.92, s32[3,1,40]{2,1,0:T(1,128)} %bitcast.93, s32[3]{0:T(128)} %bitcast.94, bf16[3,40,128,128]{3,2,1,0:T(8,128)(2,1)} %bitcast.83), custom_call_target="tpu_custom_call" | custom-call | tf_op jit(solution)/shard_map/pallas_call | solution.py:93
  8.2 2.3 %collective-permute-start.1 = (bf16[1,4,128,128]{3,2,1,0:T(8,128)(2,1)S(1)}, bf16[1,4,128,128]{3,2,1,0:T(8,128)(2,1)S(1)}, u32[]{:S(2)}, u32[]{:S(2)}) collective-permute-start(bf16[1,4,128,128]{3,2,1,0:T(8,128)(2,1)S(1)} %shard_map.96), channel_id=1, source_target_pairs={{0,4},{4,0},{8,12},{12,8},{16,20},{20,16},{24,28},{28,24},{1,5},{5... | collective-permute-start | bytes 393224 | tf_op jit(solution)/shard_map/ppermute | solution.py:238
  11.4 2.3 %collective-permute-done.1 = bf16[1,4,128,128]{3,2,1,0:T(8,128)(2,1)S(1)} collective-permute-done((bf16[1,4,128,128]{3,2,1,0:T(8,128)(2,1)S(1)}, bf16[1,4,128,128]{3,2,1,0:T(8,128)(2,1)S(1)}, u32[]{:S(2)}, u32[]{:S(2)}) %collective-permute-start.1) | collective-permute-done | bytes 131104 | tf_op jit(solution)/shard_map/ppermute | solution.py:238
  14.5 4.8 %all-to-all-start = ((bf16[4,128,128]{2,1,0:T(8,128)(2,1)}), bf16[4,128,128]{2,1,0:T(8,128)(2,1)S(1)}, u32[]{:S(2)}, u32[]{:S(2)}) async-start(bf16[4,128,128]{2,1,0:T(8,128)(2,1)} %fusion.1), calls=%async_computation | async-start | bytes 262144 | tf_op jit(solution)/shard_map/all_to_all | solution.py:248
  20.3 1.1 %collective-permute-done.2.refs_1_ = s32[16,128]{1,0:T(8,128)S(1)} collective-permute-done((s32[16,128]{1,0:T(8,128)S(1)}, s32[16,128]{1,0:T(8,128)S(1)}, u32[]{:S(2)}, u32[]{:S(2)}) %collective-permute-start.2) | collective-permute-done | bytes 8224 | tf_op jit(solution)/shard_map/ppermute | solution.py:39
  21.4 1.3 %collective-permute-done.5.refs_7_ = bf16[128,128]{1,0:T(8,128)(2,1)S(1)} collective-permute-done((bf16[128,128]{1,0:T(8,128)(2,1)S(1)}, bf16[128,128]{1,0:T(8,128)(2,1)S(1)}, u32[]{:S(2)}, u32[]{:S(2)}) %collective-permute-start.5) | collective-permute-done | bytes 32800 | tf_op jit(solution)/shard_map/ppermute | solution.py:34
  22.7 2.4 %shard_map.98 = (f32[2,4,128,128]{3,2,1,0:T(8,128)S(1)}, bf16[40,128,128]{2,1,0:T(8,128)(2,1)S(1)}) custom-call(s32[16,128]{1,0:T(8,128)S(1)} %get-tuple-element.33.refs_0_, s32[16,128]{1,0:T(8,128)S(1)} %collective-permute-done.2.refs_1_, bf16[3,40,128,128]{3,2,1,0:T(8,128)(2,1)} %bitcast.86, bf16[3,40,128,128]{3,2,1,0:T(8,128)(2,1)} %collective-permute-done.3.refs_3_, ...), custom_call_target="tpu_custom_call" | custom-call | tf_op jit(solution)/shard_map/pallas_call | solution.py:215
  26.3 1.2 %collective-permute-start.8 = (bf16[128,128]{1,0:T(8,128)(2,1)S(1)}, bf16[128,128]{1,0:T(8,128)(2,1)S(1)}, u32[]{:S(2)}, u32[]{:S(2)}) collective-permute-start(bf16[128,128]{1,0:T(8,128)(2,1)S(1)} %bitcast.73), channel_id=1, source_target_pairs={{0,3},{1,2},{2,1},{3,0},{4,7},{5,6},{6,5},{7,4},{8,11},{9,10},{10,... | collective-permute-start | bytes 98312 | tf_op jit(solution)/shard_map/ppermute | solution.py:34
  27.5 1.8 %collective-permute-done.6.refs_5_.refs_9_ = bf16[128,128]{1,0:T(8,128)(2,1)S(1)} collective-permute-done((bf16[128,128]{1,0:T(8,128)(2,1)S(1)}, bf16[128,128]{1,0:T(8,128)(2,1)S(1)}, u32[]{:S(2)}, u32[]{:S(2)}) %collective-permute-start.6) | collective-permute-done | bytes 32800 | tf_op jit(solution)/shard_map/ppermute | solution.py:34
  29.7 1.6 %shard_map.99 = bf16[1,4,128,128]{3,2,1,0:T(8,128)(2,1)S(1)} custom-call(s32[16,128]{1,0:T(8,128)S(1)} %get-tuple-element.33.refs_0_, s32[16,128]{1,0:T(8,128)S(1)} %collective-permute-done.2.refs_1_, bf16[3,40,128,128]{3,2,1,0:T(8,128)(2,1)} %bitcast.87, bf16[3,40,128,128]{3,2,1,0:T(8,128)(2,1)} %collective-permute-done.3.refs_3_, ...), custom_call_target="tpu_custom_call" | custom-call | tf_op jit(solution)/shard_map/pallas_call | solution.py:215
  31.3 1.6 %collective-permute-start.9 = (bf16[1,4,128,128]{3,2,1,0:T(8,128)(2,1)S(1)}, bf16[1,4,128,128]{3,2,1,0:T(8,128)(2,1)S(1)}, u32[]{:S(2)}, u32[]{:S(2)}) collective-permute-start(bf16[1,4,128,128]{3,2,1,0:T(8,128)(2,1)S(1)} %shard_map.99), channel_id=1, source_target_pairs={{0,4},{4,0},{8,12},{12,8},{16,20},{20,16},{24,28},{28,24},{1,5},{5... | collective-permute-start | bytes 393224 | tf_op jit(solution)/shard_map/ppermute | solution.py:238
  32.9 1.6 %shard_map.100 = f32[1,4,128,128]{3,2,1,0:T(8,128)S(1)} custom-call(s32[16,128]{1,0:T(8,128)S(1)} %get-tuple-element.33.refs_0_, s32[16,128]{1,0:T(8,128)S(1)} %collective-permute-done.2.refs_1_, bf16[3,40,128,128]{3,2,1,0:T(8,128)(2,1)} %bitcast.88, bf16[3,40,128,128]{3,2,1,0:T(8,128)(2,1)} %collective-permute-done.3.refs_3_, ...), custom_call_target="tpu_custom_call" | custom-call | tf_op jit(solution)/shard_map/pallas_call | solution.py:215
  34.5 2.6 %collective-permute-done.9 = bf16[1,4,128,128]{3,2,1,0:T(8,128)(2,1)S(1)} collective-permute-done((bf16[1,4,128,128]{3,2,1,0:T(8,128)(2,1)S(1)}, bf16[1,4,128,128]{3,2,1,0:T(8,128)(2,1)S(1)}, u32[]{:S(2)}, u32[]{:S(2)}) %collective-permute-start.9) | collective-permute-done | bytes 131104 | tf_op jit(solution)/shard_map/ppermute | solution.py:238
  37.8 5.0 %all-to-all-start.1 = ((bf16[4,128,128]{2,1,0:T(8,128)(2,1)}), bf16[4,128,128]{2,1,0:T(8,128)(2,1)S(1)}, u32[]{:S(2)}, u32[]{:S(2)}) async-start(bf16[4,128,128]{2,1,0:T(8,128)(2,1)} %fusion.2), calls=%async_computation.1 | async-start | bytes 262144 | tf_op jit(solution)/shard_map/all_to_all | solution.py:248
  42.8 3.4 %shard_map.101 = (f32[2,4,128,128]{3,2,1,0:T(8,128)S(1)}, bf16[40,128,128]{2,1,0:T(8,128)(2,1)S(1)}) custom-call(s32[16,128]{1,0:T(8,128)S(1)} %get-tuple-element.33.refs_0_, s32[16,128]{1,0:T(8,128)S(1)} %collective-permute-done.2.refs_1_, bf16[3,40,128,128]{3,2,1,0:T(8,128)(2,1)} %bitcast.89, bf16[3,40,128,128]{3,2,1,0:T(8,128)(2,1)} %collective-permute-done.3.refs_3_, ...), custom_call_target="tpu_custom_call" | custom-call | tf_op jit(solution)/shard_map/pallas_call | solution.py:215
  46.2 2.5 %all-to-all-done.1 = bf16[4,128,128]{2,1,0:T(8,128)(2,1)S(1)} async-done(((bf16[4,128,128]{2,1,0:T(8,128)(2,1)}), bf16[4,128,128]{2,1,0:T(8,128)(2,1)S(1)}, u32[]{:S(2)}, u32[]{:S(2)}) %all-to-all-start.1) | async-done | bytes 131104 | tf_op jit(solution)/shard_map/all_to_all | solution.py:248
  49.9 2.9 %collective-permute-done.10.refs_5_ = bf16[128,128]{1,0:T(8,128)(2,1)S(1)} collective-permute-done((bf16[128,128]{1,0:T(8,128)(2,1)S(1)}, bf16[128,128]{1,0:T(8,128)(2,1)S(1)}, u32[]{:S(2)}, u32[]{:S(2)}) %collective-permute-start.10) | collective-permute-done | bytes 32800 | tf_op jit(solution)/shard_map/ppermute | solution.py:34
  52.8 1.4 %shard_map.102 = bf16[1,4,128,128]{3,2,1,0:T(8,128)(2,1)S(1)} custom-call(s32[16,128]{1,0:T(8,128)S(1)} %get-tuple-element.33.refs_0_, s32[16,128]{1,0:T(8,128)S(1)} %collective-permute-done.2.refs_1_, bf16[3,40,128,128]{3,2,1,0:T(8,128)(2,1)} %bitcast.90, bf16[3,40,128,128]{3,2,1,0:T(8,128)(2,1)} %collective-permute-done.3.refs_3_, ...), custom_call_target="tpu_custom_call" | custom-call | tf_op jit(solution)/shard_map/pallas_call | solution.py:215
  54.2 2.3 %collective-permute-start.11 = (bf16[1,4,128,128]{3,2,1,0:T(8,128)(2,1)S(1)}, bf16[1,4,128,128]{3,2,1,0:T(8,128)(2,1)S(1)}, u32[]{:S(2)}, u32[]{:S(2)}) collective-permute-start(bf16[1,4,128,128]{3,2,1,0:T(8,128)(2,1)S(1)} %shard_map.102), channel_id=1, source_target_pairs={{0,4},{4,0},{8,12},{12,8},{16,20},{20,16},{24,28},{28,24},{1,5},{5... | collective-permute-start | bytes 393224 | tf_op jit(solution)/shard_map/ppermute | solution.py:238
  56.5 1.6 %shard_map.103 = f32[1,4,128,128]{3,2,1,0:T(8,128)S(1)} custom-call(s32[16,128]{1,0:T(8,128)S(1)} %get-tuple-element.33.refs_0_, s32[16,128]{1,0:T(8,128)S(1)} %collective-permute-done.2.refs_1_, bf16[3,40,128,128]{3,2,1,0:T(8,128)(2,1)} %bitcast.91, bf16[3,40,128,128]{3,2,1,0:T(8,128)(2,1)} %collective-permute-done.3.refs_3_, ...), custom_call_target="tpu_custom_call" | custom-call | tf_op jit(solution)/shard_map/pallas_call | solution.py:215
  58.1 1.3 %collective-permute-done.11 = bf16[1,4,128,128]{3,2,1,0:T(8,128)(2,1)S(1)} collective-permute-done((bf16[1,4,128,128]{3,2,1,0:T(8,128)(2,1)S(1)}, bf16[1,4,128,128]{3,2,1,0:T(8,128)(2,1)S(1)}, u32[]{:S(2)}, u32[]{:S(2)}) %collective-permute-start.11) | collective-permute-done | bytes 131104 | tf_op jit(solution)/shard_map/ppermute | solution.py:238
  60.1 3.3 %all-to-all-start.2 = ((bf16[4,128,128]{2,1,0:T(8,128)(2,1)}), bf16[4,128,128]{2,1,0:T(8,128)(2,1)S(1)}, u32[]{:S(2)}, u32[]{:S(2)}) async-start(bf16[4,128,128]{2,1,0:T(8,128)(2,1)} %fusion.3), calls=%async_computation.2 | async-start | bytes 262144 | tf_op jit(solution)/shard_map/all_to_all | solution.py:248
  64.1 5.2 %all-to-all-done.2 = bf16[4,128,128]{2,1,0:T(8,128)(2,1)S(1)} async-done(((bf16[4,128,128]{2,1,0:T(8,128)(2,1)}), bf16[4,128,128]{2,1,0:T(8,128)(2,1)S(1)}, u32[]{:S(2)}, u32[]{:S(2)}) %all-to-all-start.2) | async-done | bytes 131104 | tf_op jit(solution)/shard_map/all_to_all | solution.py:248
  (35 shorter events, 10.6 us)
Async XLA Ops:
  0.6 22.1 %collective-permute-start.3 = (bf16[3,40,128,128]{3,2,1,0:T(8,128)(2,1)}, bf16[3,40,128,128]{3,2,1,0:T(8,128)(2,1)}, u32[]{:S(2)}, u32[]{:S(2)}) collective-permute-start(bf16[3,40,128,128]{3,2,1,0:T(8,128)(2,1)} %bitcast.82), channel_id=1, source_target_pairs={{0,1},{1,0},{2,3},{3,2},{4,5},{5,4},{6,7},{7,6},{8,9},{9,8},{10,11... | collective-permute-start | bytes 11796488 | tf_op jit(solution)/shard_map/ppermute | solution.py:39
  2.0 5.1 %collective-permute-start = (bf16[128,128]{1,0:T(8,128)(2,1)S(1)}, bf16[128,128]{1,0:T(8,128)(2,1)S(1)}, u32[]{:S(2)}, u32[]{:S(2)}) collective-permute-start(bf16[128,128]{1,0:T(8,128)(2,1)S(1)} %convolution_convert_fusion.3.refs_2_.refs_4_), channel_id=1, source_target_pairs={{0,2},{1,3},{2,0},{3,1},{4,6},{5,7},{6,4},{7,5},{8,10},{9,11},{10,... | collective-permute-start | bytes 98312 | tf_op jit(solution)/shard_map/ppermute | solution.py:34
  8.2 5.6 %collective-permute-start.1 = (bf16[1,4,128,128]{3,2,1,0:T(8,128)(2,1)S(1)}, bf16[1,4,128,128]{3,2,1,0:T(8,128)(2,1)S(1)}, u32[]{:S(2)}, u32[]{:S(2)}) collective-permute-start(bf16[1,4,128,128]{3,2,1,0:T(8,128)(2,1)S(1)} %shard_map.96), channel_id=1, source_target_pairs={{0,4},{4,0},{8,12},{12,8},{16,20},{20,16},{24,28},{28,24},{1,5},{5... | collective-permute-start | bytes 393224 | tf_op jit(solution)/shard_map/ppermute | solution.py:238
  14.5 10.7 %all-to-all-start = ((bf16[4,128,128]{2,1,0:T(8,128)(2,1)}), bf16[4,128,128]{2,1,0:T(8,128)(2,1)S(1)}, u32[]{:S(2)}, u32[]{:S(2)}) async-start(bf16[4,128,128]{2,1,0:T(8,128)(2,1)} %fusion.1), calls=%async_computation | async-start | bytes 262144 | tf_op jit(solution)/shard_map/all_to_all | solution.py:248
  19.3 5.9 %copy-start = (bf16[1,1,1,2,128,128]{5,4,3,2,1,0:T(8,128)(2,1)S(1)}, bf16[1,1,1,2,128,128]{5,4,3,2,1,0:T(8,128)(2,1)}, u32[]{:S(2)}) copy-start(bf16[1,1,1,2,128,128]{5,4,3,2,1,0:T(8,128)(2,1)} %param.12) | copy-start | bytes 196612
  19.3 6.0 %copy-start.1 = (bf16[1,1,1,2,128,128]{5,4,3,2,1,0:T(8,128)(2,1)S(1)}, bf16[1,1,1,2,128,128]{5,4,3,2,1,0:T(8,128)(2,1)}, u32[]{:S(2)}) copy-start(bf16[1,1,1,2,128,128]{5,4,3,2,1,0:T(8,128)(2,1)} %param.14) | copy-start | bytes 196612
  19.3 2.1 %collective-permute-start.4 = (bf16[128,128]{1,0:T(8,128)(2,1)S(1)}, bf16[128,128]{1,0:T(8,128)(2,1)S(1)}, u32[]{:S(2)}, u32[]{:S(2)}) collective-permute-start(bf16[128,128]{1,0:T(8,128)(2,1)S(1)} %convolution_convert_fusion.3.refs_2_.refs_4_), channel_id=1, source_target_pairs={{0,1},{1,0},{2,3},{3,2},{4,5},{5,4},{6,7},{7,6},{8,9},{9,8},{10,11... | collective-permute-start | bytes 98312 | tf_op jit(solution)/shard_map/ppermute | solution.py:34
  19.3 3.4 %collective-permute-start.5 = (bf16[128,128]{1,0:T(8,128)(2,1)S(1)}, bf16[128,128]{1,0:T(8,128)(2,1)S(1)}, u32[]{:S(2)}, u32[]{:S(2)}) collective-permute-start(bf16[128,128]{1,0:T(8,128)(2,1)S(1)} %convolution_convert_fusion.3.refs_2_.refs_4_), channel_id=1, source_target_pairs={{0,3},{1,2},{2,1},{3,0},{4,7},{5,6},{6,5},{7,4},{8,11},{9,10},{10,... | collective-permute-start | bytes 98312 | tf_op jit(solution)/shard_map/ppermute | solution.py:34
  20.2 1.2 %collective-permute-start.2 = (s32[16,128]{1,0:T(8,128)S(1)}, s32[16,128]{1,0:T(8,128)S(1)}, u32[]{:S(2)}, u32[]{:S(2)}) collective-permute-start(s32[16,128]{1,0:T(8,128)S(1)} %get-tuple-element.33.refs_0_), channel_id=1, source_target_pairs={{0,1},{1,0},{2,3},{3,2},{4,5},{5,4},{6,7},{7,6},{8,9},{9,8},{10,11... | collective-permute-start | bytes 24584 | tf_op jit(solution)/shard_map/ppermute | solution.py:39
  25.4 3.9 %collective-permute-start.6 = (bf16[128,128]{1,0:T(8,128)(2,1)S(1)}, bf16[128,128]{1,0:T(8,128)(2,1)S(1)}, u32[]{:S(2)}, u32[]{:S(2)}) collective-permute-start(bf16[128,128]{1,0:T(8,128)(2,1)S(1)} %bitcast.71), channel_id=1, source_target_pairs={{0,2},{1,3},{2,0},{3,1},{4,6},{5,7},{6,4},{7,5},{8,10},{9,11},{10,... | collective-permute-start | bytes 98312 | tf_op jit(solution)/shard_map/ppermute | solution.py:34
  26.2 3.1 %collective-permute-start.7 = (bf16[128,128]{1,0:T(8,128)(2,1)S(1)}, bf16[128,128]{1,0:T(8,128)(2,1)S(1)}, u32[]{:S(2)}, u32[]{:S(2)}) collective-permute-start(bf16[128,128]{1,0:T(8,128)(2,1)S(1)} %bitcast.72), channel_id=1, source_target_pairs={{0,1},{1,0},{2,3},{3,2},{4,5},{5,4},{6,7},{7,6},{8,9},{9,8},{10,11... | collective-permute-start | bytes 98312 | tf_op jit(solution)/shard_map/ppermute | solution.py:34
  26.3 3.4 %collective-permute-start.8 = (bf16[128,128]{1,0:T(8,128)(2,1)S(1)}, bf16[128,128]{1,0:T(8,128)(2,1)S(1)}, u32[]{:S(2)}, u32[]{:S(2)}) collective-permute-start(bf16[128,128]{1,0:T(8,128)(2,1)S(1)} %bitcast.73), channel_id=1, source_target_pairs={{0,3},{1,2},{2,1},{3,0},{4,7},{5,6},{6,5},{7,4},{8,11},{9,10},{10,... | collective-permute-start | bytes 98312 | tf_op jit(solution)/shard_map/ppermute | solution.py:34
  31.3 5.8 %collective-permute-start.9 = (bf16[1,4,128,128]{3,2,1,0:T(8,128)(2,1)S(1)}, bf16[1,4,128,128]{3,2,1,0:T(8,128)(2,1)S(1)}, u32[]{:S(2)}, u32[]{:S(2)}) collective-permute-start(bf16[1,4,128,128]{3,2,1,0:T(8,128)(2,1)S(1)} %shard_map.99), channel_id=1, source_target_pairs={{0,4},{4,0},{8,12},{12,8},{16,20},{20,16},{24,28},{28,24},{1,5},{5... | collective-permute-start | bytes 393224 | tf_op jit(solution)/shard_map/ppermute | solution.py:238
  37.8 10.9 %all-to-all-start.1 = ((bf16[4,128,128]{2,1,0:T(8,128)(2,1)}), bf16[4,128,128]{2,1,0:T(8,128)(2,1)S(1)}, u32[]{:S(2)}, u32[]{:S(2)}) async-start(bf16[4,128,128]{2,1,0:T(8,128)(2,1)} %fusion.2), calls=%async_computation.1 | async-start | bytes 262144 | tf_op jit(solution)/shard_map/all_to_all | solution.py:248
  42.8 5.9 %copy-start.2 = (bf16[1,1,2,128,128]{4,3,2,1,0:T(8,128)(2,1)S(1)}, bf16[1,1,2,128,128]{4,3,2,1,0:T(8,128)(2,1)}, u32[]{:S(2)}) copy-start(bf16[1,1,2,128,128]{4,3,2,1,0:T(8,128)(2,1)} %param.15) | copy-start | bytes 196612
  42.8 6.0 %copy-start.3 = (bf16[1,1,2,128,128]{4,3,2,1,0:T(8,128)(2,1)S(1)}, bf16[1,1,2,128,128]{4,3,2,1,0:T(8,128)(2,1)}, u32[]{:S(2)}) copy-start(bf16[1,1,2,128,128]{4,3,2,1,0:T(8,128)(2,1)} %param.13) | copy-start | bytes 196612
  48.9 3.9 %collective-permute-start.10 = (bf16[128,128]{1,0:T(8,128)(2,1)S(1)}, bf16[128,128]{1,0:T(8,128)(2,1)S(1)}, u32[]{:S(2)}, u32[]{:S(2)}) collective-permute-start(bf16[128,128]{1,0:T(8,128)(2,1)S(1)} %bitcast.78), channel_id=1, source_target_pairs={{0,2},{1,3},{2,0},{3,1},{4,6},{5,7},{6,4},{7,5},{8,10},{9,11},{10,... | collective-permute-start | bytes 98312 | tf_op jit(solution)/shard_map/ppermute | solution.py:34
  54.2 5.2 %collective-permute-start.11 = (bf16[1,4,128,128]{3,2,1,0:T(8,128)(2,1)S(1)}, bf16[1,4,128,128]{3,2,1,0:T(8,128)(2,1)S(1)}, u32[]{:S(2)}, u32[]{:S(2)}) collective-permute-start(bf16[1,4,128,128]{3,2,1,0:T(8,128)(2,1)S(1)} %shard_map.102), channel_id=1, source_target_pairs={{0,4},{4,0},{8,12},{12,8},{16,20},{20,16},{24,28},{28,24},{1,5},{5... | collective-permute-start | bytes 393224 | tf_op jit(solution)/shard_map/ppermute | solution.py:238
  60.1 9.2 %all-to-all-start.2 = ((bf16[4,128,128]{2,1,0:T(8,128)(2,1)}), bf16[4,128,128]{2,1,0:T(8,128)(2,1)S(1)}, u32[]{:S(2)}, u32[]{:S(2)}) async-start(bf16[4,128,128]{2,1,0:T(8,128)(2,1)} %fusion.3), calls=%async_computation.2 | async-start | bytes 262144 | tf_op jit(solution)/shard_map/all_to_all | solution.py:248
